TPU v7x, 32 devices: a whole 2x2x4 slice. The times are simulated.
32 devices in a mesh: groups: 2 (over y), flat: 4 (over z), dp: 4 (over x, core).
Axes of the slice: x: 2, y: 2, z: 4, core: 2. Of those that a mesh axis runs over, the one named last changes fastest.
Arguments:
- activations: bfloat16 [4096, 14336], P(('groups', 'dp'), 'flat'), parts along dimension 0
- curvature: float32 [4096], P(('groups', 'dp')), parts along dimension 0, may hold values from 0.3 to 3
- vector_now: float32 [28672, 4096], P(('groups', 'flat', 'dp')), parts along dimension 0
- vector_before: float32 [28672, 4096], P(('groups', 'flat', 'dp')), parts along dimension 0, may hold values from -6 to 6
- sign_bits: int32 [28672, 4096], P(('groups', 'flat', 'dp')), parts along dimension 0, may hold values from 0 to 1
- prior_precision: float32 [2], P('groups'), parts along dimension 0, may hold values from 0.2 to 2
- beta_before: float32 [2], P('groups'), parts along dimension 0, may hold values from 0.3 to 1.5
- kept_rows: int32 [8192], P('groups'), parts along dimension 0, may hold values from 0 to 3583
- kept_cols: int32 [8192], P('groups'), parts along dimension 0, may hold values from 0 to 16383
Outputs:
- vector_next: float32 [28672, 4096], P(('groups', 'flat', 'dp')), parts along dimension 0
- alpha_value: float32 [2], P('groups'), parts along dimension 0
- beta_value: float32 [2], P('groups'), parts along dimension 0
- sketch: float32 [8192], P('groups'), parts along dimension 0
There are 2 independent parts, one for each index of `groups`. A program takes and returns all parts, laid end to end along the dimension named above; each array names one. Nothing has to cross between parts.
All inputs are finite; a program needn't handle non-finite values.
Results may differ from a plain program's by a relative error of at most 0.015.
Values may be sent and summed in bfloat16 or wider, within the bound.
A program may use at most 256 MiB of HBM per device.

v0:
```python
import math
import jax
import jax.numpy as jnp
from jax import lax
from jax.sharding import PartitionSpec as P

BLOCK = 128


def parity_sign(row_index, col_index):
    common_bits = jnp.bitwise_and(row_index, col_index)
    parity_sum = jnp.zeros_like(common_bits)
    for position in range(BLOCK.bit_length() - 1):
        parity_sum = parity_sum + jnp.bitwise_and(jnp.right_shift(common_bits, position), 1)
    return (1 - 2 * jnp.bitwise_and(parity_sum, 1)).astype(jnp.float32) / math.sqrt(BLOCK)


def hadamard_table():
    row_index = lax.broadcasted_iota(jnp.int32, (BLOCK, BLOCK), 0)
    col_index = lax.broadcasted_iota(jnp.int32, (BLOCK, BLOCK), 1)
    return parity_sign(row_index, col_index)


def pick_dense(column_block, hadamard, own_index, kept_rows, kept_cols):
    cols_here = column_block.shape[1]
    section_two = jnp.einsum(
        "ri,bic->brc",
        hadamard,
        column_block.reshape(-1, BLOCK, cols_here),
        precision=lax.Precision.HIGHEST,
    )
    section_two = section_two.reshape(-1, cols_here)
    first_col = own_index * cols_here
    inside = jnp.logical_and(kept_cols >= first_col, kept_cols < first_col + cols_here)
    local_col = jnp.clip(kept_cols - first_col, 0, cols_here - 1)
    return jnp.where(inside, section_two[kept_rows, local_col], 0.0)


def on_device(
    activations,
    curvature,
    vector_now,
    vector_before,
    sign_bits,
    prior_precision,
    beta_before,
    kept_rows,
    kept_cols,
):
    token_count = activations.shape[0]
    out_width = vector_now.shape[1]
    local_rows = vector_now.shape[0]
    flat_count = lax.axis_size("flat")
    data_count = lax.axis_size("dp")
    total_tokens = token_count * data_count
    total_cells = local_rows * out_width * flat_count * data_count
    vector_half = vector_now.astype(jnp.bfloat16)
    columns = activations
    partial_out = jnp.dot(
        columns,
        lax.all_gather(vector_half, "dp", axis=0, tiled=True),
        preferred_element_type=jnp.float32,
    )
    shares = lax.psum_scatter(
        partial_out.astype(jnp.bfloat16), "flat", scatter_dimension=1, tiled=True
    ).astype(jnp.float32)
    scaled_share = (curvature[:, None] * shares / total_tokens).astype(jnp.bfloat16)
    scaled = lax.all_gather(scaled_share, "flat", axis=1, tiled=True)
    columns = activations
    image_data = lax.psum_scatter(
        lax.dot_general(
            columns, scaled, (((0,), (0,)), ((), ())), preferred_element_type=jnp.float32
        ).astype(jnp.bfloat16),
        "dp",
        scatter_dimension=0,
        tiled=True,
    ).astype(jnp.float32)
    new_image = image_data + prior_precision[0] * vector_now
    beta_old = beta_before[0]
    alpha_value = lax.psum(jnp.sum(new_image * vector_now), ("flat", "dp")) / total_cells
    residual = new_image - alpha_value * vector_now - beta_old * vector_before
    square = lax.psum(jnp.sum(residual * residual), ("flat", "dp")) / total_cells
    beta_value = jnp.sqrt(square + 1e-06)
    vector_next = residual / beta_value
    hadamard = hadamard_table()
    signed = (2 * sign_bits - 1).astype(jnp.float32) * vector_next
    rows_here = local_rows * out_width // (BLOCK * BLOCK)
    section_one = jnp.dot(signed.reshape(-1, BLOCK), hadamard, precision=lax.Precision.HIGHEST)
    section_one = section_one.reshape(rows_here, BLOCK * BLOCK)
    own_index = lax.axis_index(("flat", "dp"))
    column_block = lax.all_to_all(
        section_one.astype(jnp.bfloat16), ("flat", "dp"), split_axis=1, concat_axis=0, tiled=True
    ).astype(section_one.dtype)
    local_values = pick_dense(column_block, hadamard, own_index, kept_rows, kept_cols)
    sketch = lax.psum(local_values, ("flat", "dp"))
    return (vector_next, alpha_value.reshape(1), beta_value.reshape(1), sketch)


def solution(mesh):
    placed = (
        P(("groups", "dp"), "flat"),
        P(("groups", "dp")),
        P(("groups", "flat", "dp"), None),
        P(("groups", "flat", "dp"), None),
        P(("groups", "flat", "dp"), None),
        P("groups"),
        P("groups"),
        P("groups"),
        P("groups"),
    )
    return jax.shard_map(
        on_device,
        mesh=mesh,
        in_specs=placed,
        out_specs=(P(("groups", "flat", "dp"), None), P("groups"), P("groups"), P("groups")),
        check_vma=False,
    )
```

profile of v0, /device:TPU:0, one launch (start us, length us, event | category | flops | bytes accessed | tf_op | source)
XLA Modules:
  0.0 1159.3 jit_solution(15920801584408900253)
XLA Ops:
  7.2 9.4 convert_element_type.37
  16.6 0.0 reduce-scatter.5.cloned.1.call-start
  16.7 180.8 %all-gather.3.cloned.1.call-done = bf16[3584,4096]{1,0:T(8,128)(2,1)} async-done(((bf16[896,4096]{1,0:T(8,128)(2,1)}), bf16[3584,4096]{1,0:T(8,128)(2,1)}) %all-gather.3.cloned.1.call-update) | async-done | bytes 29360144 | tf_op jit(solution)/shard_map/all_gather | solution.py:61
  197.4 23.0 %convolution_convert_fusion.2 = bf16[512,4096]{1,0:T(8,128)(2,1)} fusion(bf16[512,3584]{1,0:T(8,128)(2,1)} %param.9, bf16[3584,4096]{1,0:T(8,128)(2,1)} %all-gather.3.cloned.1.call-done), kind=kOutput, calls=%fused_computation.10 | convolution fusion | flops 15034482688 | bytes 37224448 | tf_op jit(solution)/shard_map/dot_general | solution.py:59
  220.5 0.0 all-gather.5.cloned.1.call-start
  220.5 76.9 %reduce-scatter.5.cloned.1.call-done = bf16[512,1024]{1,0:T(8,128)(2,1)} async-done(((bf16[512,4096]{1,0:T(8,128)(2,1)}), bf16[512,1024]{1,0:T(8,128)(2,1)}) %reduce-scatter.5.cloned.1.call-update) | async-done | bytes 1048592 | tf_op jit(solution)/shard_map/reduce_scatter | solution.py:64
  297.4 2.5 multiply_convert_fusion
  299.9 0.2 reduce-scatter.7.cloned.1.call-start
  300.2 81.2 %all-gather.5.cloned.1.call-done = bf16[512,4096]{1,0:T(8,128)(2,1)} async-done(((bf16[512,1024]{1,0:T(8,128)(2,1)}), bf16[512,4096]{1,0:T(8,128)(2,1)}) %all-gather.5.cloned.1.call-update) | async-done | bytes 4194320 | tf_op jit(solution)/shard_map/all_gather | solution.py:68
  381.4 22.3 %fusion = bf16[3584,4096]{0,1:T(8,128)(2,1)} fusion(bf16[512,4096]{1,0:T(8,128)(2,1)} %all-gather.5.cloned.1.call-done, bf16[512,3584]{1,0:T(8,128)(2,1)} %param.9), kind=kOutput, calls=%fused_computation.3 | convolution fusion | flops 15047065600 | bytes 37224448 | tf_op jit(solution)/shard_map/dot_general | solution.py:71
  403.7 37.0 %copy.36 = bf16[3584,4096]{1,0:T(8,128)(2,1)} copy(bf16[3584,4096]{0,1:T(8,128)(2,1)} %fusion) | data formatting | bytes 58720256
  440.7 16.7 %copy.28 = f32[896,4096]{0,1:T(8,128)} copy(f32[896,4096]{1,0:T(8,128)} %param.11) | data formatting | bytes 29360128 | tf_op args[2]
  458.1 18.0 %copy.31 = f32[896,4096]{0,1:T(8,128)} copy(f32[896,4096]{1,0:T(8,128)} %param.12) | data formatting | bytes 29360128 | tf_op args[3]
  476.1 171.1 %reduce-scatter.7.cloned.1.call-done = bf16[896,4096]{1,0:T(8,128)(2,1)} async-done(((bf16[3584,4096]{1,0:T(8,128)(2,1)}), bf16[896,4096]{1,0:T(8,128)(2,1)}) %reduce-scatter.7.cloned.1.call-update) | async-done | bytes 7340048
  647.2 10.8 copy.37
  658.1 11.6 %multiply_reduce_fusion.1 = f32[]{:T(128)} fusion(f32[896,4096]{0,1:T(8,128)} %copy.28, bf16[896,4096]{0,1:T(8,128)(2,1)} %copy.37, f32[]{:T(128)} %bitcast.22), kind=kLoop, calls=%fused_computation.7 | loop fusion | flops 18350080 | bytes 22020104 | tf_op jit(solution)/shard_map/reduce_sum | solution.py:80
  670.4 32.9 %psum.21 = f32[]{:T(128)} all-reduce(f32[]{:T(128)} %multiply_reduce_fusion.1), channel_id=1, replica_groups=mesh['groups'=2,'flat'=4,'dp'=4] {'flat','dp'}, use_global_device_ids=true, to_apply=%region_3.0 | all-reduce | flops 1 | bytes 8 | tf_op jit(solution)/shard_map/psum | solution.py:80
  703.9 13.4 %multiply_reduce_fusion = f32[]{:T(128)} fusion(f32[896,4096]{0,1:T(8,128)} %copy.31, f32[]{:T(128)} %bitcast.25, f32[896,4096]{0,1:T(8,128)} %copy.28, f32[]{:T(128)} %div.28, f32[]{:T(128)} %bitcast.23, bf16[896,4096]{0,1:T(8,128)(2,1)} %copy.37), kind=kLoop, calls=%fused_computation.5 | loop fusion | flops 33030144 | bytes 36700176 | tf_op jit(solution)/shard_map/reduce_sum | solution.py:82
  717.3 16.1 %copy.32 = s32[896,4096]{0,1:T(8,128)} copy(s32[896,4096]{1,0:T(8,128)} %param.13) | data formatting | bytes 29360128 | tf_op args[4]
  733.4 30.3 %psum.22 = f32[]{:T(128)} all-reduce(f32[]{:T(128)} %multiply_reduce_fusion), channel_id=1, replica_groups=mesh['groups'=2,'flat'=4,'dp'=4] {'flat','dp'}, use_global_device_ids=true, to_apply=%region_5.0 | all-reduce | flops 1 | bytes 8 | tf_op jit(solution)/shard_map/psum | solution.py:82
  764.4 28.3 %convert_multiply_fusion = (f32[896,4096]{0,1:T(8,128)}, f32[896,4096]{0,1:T(8,128)}) fusion(s32[896,4096]{0,1:T(8,128)} %copy.32, f32[]{:T(128)} %sqrt.3, f32[896,4096]{0,1:T(8,128)} %copy.31, f32[]{:T(128)} %bitcast.26, f32[896,4096]{0,1:T(8,128)} %copy.28, f32[]{:T(128)} %div.28, f32[]{:T(128)} %bitcast.24, bf16[896,4096]{0,1:T(8,128)(2,1)} %copy.37), kind=kLoop, calls=%fused_computation.4 | loop fusion | flops 44040192 | bytes 80740368 | tf_op jit(solution)/shard_map/mul | solution.py:86
  792.7 16.1 %copy.33 = f32[896,4096]{1,0:T(8,128)} copy(f32[896,4096]{0,1:T(8,128)} %get-tuple-element.16) | data formatting | bytes 29360128 | tf_op jit(solution)/shard_map/mul | solution.py:86
  808.8 15.8 %reshape.33 = f32[28672,128]{1,0:T(8,128)} reshape(f32[896,4096]{1,0:T(8,128)} %copy.33) | data formatting | bytes 29360128 | tf_op jit(solution)/shard_map/reshape | solution.py:88
  824.6 15.6 %convolution_convert_fusion = bf16[28672,128]{1,0:T(8,128)(2,1)} fusion(f32[28672,128]{1,0:T(8,128)} %reshape.33), kind=kOutput, calls=%fused_computation.1 | convolution fusion | flops 5641240576 | bytes 22020096 | tf_op jit(solution)/shard_map/dot_general | solution.py:88
  840.3 11.8 %convert_element_type.47 = bf16[224,16,1024]{2,1,0:T(8,128)(2,1)} reshape(bf16[28672,128]{1,0:T(8,128)(2,1)} %convolution_convert_fusion) | data formatting | bytes 14680064 | tf_op jit(solution)/shard_map/convert_element_type | solution.py:92
  852.0 10.2 copy.34
  862.2 5.0 all-to-all-start
  867.2 16.1 %copy.35 = f32[896,4096]{1,0:T(8,128)} copy(f32[896,4096]{0,1:T(8,128)} %get-tuple-element.17) | data formatting | bytes 29360128
  883.3 116.0 %all-to-all-done = bf16[224,16,1024]{2,0,1:T(8,128)(2,1)} async-done(((bf16[224,16,1024]{2,0,1:T(8,128)(2,1)}), bf16[224,16,1024]{2,0,1:T(8,128)(2,1)}, u32[]{:S(2)}, u32[]{:S(2)}) %all-to-all-start) | async-done | bytes 7340064 | tf_op jit(solution)/shard_map/all_to_all | solution.py:91
  999.3 12.7 %fusion.1 = f32[28,1024,128]{1,2,0:T(8,128)} fusion(bf16[28,128,1024]{2,1,0:T(8,128)(2,1)} %bitcast.6), kind=kOutput, calls=%fused_computation.12 | convolution fusion | flops 5637570560 | bytes 22020096 | tf_op jit(solution)/shard_map/ri,bic->brc/dot_general | solution.py:26
  1012.0 50.1 %gather_fusion = f32[4096]{0:T(1024)S(1)} fusion(f32[3584,1024]{1,0:T(8,128)} %bitcast.27, s32[4096]{0:T(1024)S(1)} %fusion.5), kind=kCustom, calls=%fused_computation | custom fusion | bytes 65536 | tf_op jit(solution)/shard_map/gather | solution.py:36
  1062.1 88.3 %psum.23 = f32[4096]{0:T(1024)} all-reduce(f32[4096]{0:T(1024)S(1)} %and_select_fusion), channel_id=1, replica_groups=mesh['groups'=2,'flat'=4,'dp'=4] {'flat','dp'}, use_global_device_ids=true, to_apply=%region_6.7 | all-reduce | flops 4096 | bytes 32768 | tf_op jit(solution)/shard_map/psum | solution.py:95
  (13 shorter events, 0.1 us)
Async XLA Ops:
  7.2 190.3 %all-gather.3.cloned.1.call-start = ((), (), s32[]{:S(2)}) async-start(), calls=%async_computation.3 | async-start | bytes 36700160 | tf_op jit(solution)/shard_map/all_gather | solution.py:61
  16.6 280.8 %copy-start.2 = (f32[512]{0:T(512)S(1)}, f32[512]{0:T(512)}, u32[]{:S(2)}) copy-start(f32[512]{0:T(512)} %param.10) | copy-start | bytes 6148
  16.6 280.8 %reduce-scatter.5.cloned.1.call-start = ((), (), s32[]{:S(2)}) async-start(), calls=%async_computation.4 | async-start | bytes 5242880 | tf_op jit(solution)/shard_map/reduce_scatter | solution.py:64
  220.5 160.9 %all-gather.5.cloned.1.call-start = ((), (), s32[]{:S(2)}) async-start(), calls=%async_computation.5 | async-start | bytes 5242880 | tf_op jit(solution)/shard_map/all_gather | solution.py:68
  299.9 347.3 %reduce-scatter.7.cloned.1.call-start = ((), (), s32[]{:S(2)}) async-start(), calls=%async_computation.6 | async-start | bytes 36700160
  852.0 15.2 %copy-start = (s32[4096]{0:T(1024)S(1)}, s32[4096]{0:T(1024)}, u32[]{:S(2)}) copy-start(s32[4096]{0:T(1024)} %param.17) | copy-start | bytes 49156
  852.0 15.2 %copy-start.1 = (s32[4096]{0:T(1024)S(1)}, s32[4096]{0:T(1024)}, u32[]{:S(2)}) copy-start(s32[4096]{0:T(1024)} %param.16) | copy-start | bytes 49156
  862.2 137.1 %all-to-all-start = ((bf16[224,16,1024]{2,0,1:T(8,128)(2,1)}), bf16[224,16,1024]{2,0,1:T(8,128)(2,1)}, u32[]{:S(2)}, u32[]{:S(2)}) async-start(bf16[224,16,1024]{2,0,1:T(8,128)(2,1)} %copy.34), calls=%async_computation.1 | async-start | bytes 14680064 | tf_op jit(solution)/shard_map/all_to_all | solution.py:91
Sparse Core Ops, SparseCore 0:
  16.7 180.6 all-gather.2
  220.6 76.7 reduce-scatter.4
  300.1 81.2 all-gather.4
  440.8 206.3 reduce-scatter.6
where the time goes:
time: 1160 us
  waiting for transfers between devices  626 us (54%)
  local copies, waits for them, and re-layouts  219 us (19%)
  blocking collectives  152 us (13%)
  matrix products  73.6 us (6%)
  other arithmetic  65.2 us (6%)
  between operations  18.8 us (2%)
    all_gather x1, waiting for transfers between devices, on_device(): lax.all_gather(vector_half, 'dp', axis=0, tiled=True)  181 us
    unnamed x5, waiting for transfers between devices  171 us
    all_to_all x1, waiting for transfers between devices, on_device(): lax.all_to_all(section_one.astype(jnp.bfloat16), ('flat', 'dp'), split_ax...  116 us
    unnamed x12, local copies, waits for them, and re-layouts  115 us
    psum x1, blocking collectives, on_device(): sketch = lax.psum(local_values, ('flat', 'dp'))  88.3 us
    all_gather x1, waiting for transfers between devices, on_device(): scaled = lax.all_gather(scaled_share, 'flat', axis=1, tiled=True)  81.2 us
    reduce_scatter x1, waiting for transfers between devices, on_device(): lax.psum_scatter(partial_out.astype(jnp.bfloat16), 'flat', scatter_dimens...  76.9 us
    gather x1, local copies, waits for them, and re-layouts, pick_dense(): return jnp.where(inside, section_two[kept_rows, local_col], 0.0)  50.1 us
  transfers between devices with their start and end apart: 5, of which 5 were waited for; matrix products, arithmetic and copies ran while one was open for 4% of the time, Pallas kernels for 0%

commit v1 on v0

--- a/solution.py
+++ b/solution.py
@@ -5,6 +5,12 @@
 from jax.sharding import PartitionSpec as P
 
 BLOCK = 128
+
+
+def summed_here(x, name):
+    pieces = lax.all_gather(x, name, axis=0, tiled=False)
+    total = pieces.sum(axis=0)
+    return total
 
 
 def parity_sign(row_index, col_index):
@@ -92,7 +98,7 @@
         section_one.astype(jnp.bfloat16), ("flat", "dp"), split_axis=1, concat_axis=0, tiled=True
     ).astype(section_one.dtype)
     local_values = pick_dense(column_block, hadamard, own_index, kept_rows, kept_cols)
-    sketch = lax.psum(local_values, ("flat", "dp"))
+    sketch = summed_here(local_values, ("flat", "dp"))
     return (vector_next, alpha_value.reshape(1), beta_value.reshape(1), sketch)
 
 

time: 1160 us -> 1130 us (0.974)
  blocking collectives: 152 us -> 112 us
    psum x1 -> x0, blocking collectives: 88.3 us -> none  [on_device(): sketch = lax.psum(local_values, ('flat', 'dp'))]
    all_gather x0 -> x1, blocking collectives: none -> 48.9 us  [summed_here(): pieces = lax.all_gather(x, name, axis=0, tiled=False)]
  transfers between devices with their start and end apart: 5 -> 5, of which waited for: 5 -> 5; matrix products, arithmetic and copies ran while one was open for 4% -> 5% of each run, Pallas kernels for 0% -> 0%
where the time goes in v1:
time: 1130 us; the launch traced here: 1120 us
  waiting for transfers between devices  626 us (55%)
  local copies, waits for them, and re-layouts  219 us (19%)
  blocking collectives  112 us (10%)
  matrix products  73.6 us (7%)
  other arithmetic  65.8 us (6%)
  between operations  18.8 us (2%)
    all_gather x1, waiting for transfers between devices, on_device(): lax.all_gather(vector_half, 'dp', axis=0, tiled=True)  181 us
    unnamed x5, waiting for transfers between devices  171 us
    all_to_all x1, waiting for transfers between devices, on_device(): lax.all_to_all(section_one.astype(jnp.bfloat16), ('flat', 'dp'), split_ax...  116 us
    unnamed x12, local copies, waits for them, and re-layouts  115 us
    all_gather x1, waiting for transfers between devices, on_device(): scaled = lax.all_gather(scaled_share, 'flat', axis=1, tiled=True)  81.2 us
    reduce_scatter x1, waiting for transfers between devices, on_device(): lax.psum_scatter(partial_out.astype(jnp.bfloat16), 'flat', scatter_dimens...  76.9 us
    gather x1, local copies, waits for them, and re-layouts, pick_dense(): return jnp.where(inside, section_two[kept_rows, local_col], 0.0)  50.1 us
    all_gather x1, blocking collectives, summed_here(): pieces = lax.all_gather(x, name, axis=0, tiled=False)  48.9 us
  transfers between devices with their start and end apart: 5, of which 5 were waited for; matrix products, arithmetic and copies ran while one was open for 5% of the time, Pallas kernels for 0%

profile of v1, /device:TPU:0, one launch (start us, length us, event | category | flops | bytes accessed | tf_op | source)
XLA Modules:
  0.0 1120.5 jit_solution(626506620005076519)
XLA Ops:
  7.2 9.4 convert_element_type.37
  16.7 180.8 %all-gather.4.cloned.1.call-done = bf16[3584,4096]{1,0:T(8,128)(2,1)} async-done(((bf16[896,4096]{1,0:T(8,128)(2,1)}), bf16[3584,4096]{1,0:T(8,128)(2,1)}) %all-gather.4.cloned.1.call-update) | async-done | bytes 29360144 | tf_op jit(solution)/shard_map/all_gather | solution.py:67
  197.4 23.0 %convolution_convert_fusion.2 = bf16[512,4096]{1,0:T(8,128)(2,1)} fusion(bf16[512,3584]{1,0:T(8,128)(2,1)} %param.9, bf16[3584,4096]{1,0:T(8,128)(2,1)} %all-gather.4.cloned.1.call-done), kind=kOutput, calls=%fused_computation.10 | convolution fusion | flops 15034482688 | bytes 37224448 | tf_op jit(solution)/shard_map/dot_general | solution.py:65
  220.5 76.9 %reduce-scatter.5.cloned.1.call-done = bf16[512,1024]{1,0:T(8,128)(2,1)} async-done(((bf16[512,4096]{1,0:T(8,128)(2,1)}), bf16[512,1024]{1,0:T(8,128)(2,1)}) %reduce-scatter.5.cloned.1.call-update) | async-done | bytes 1048592 | tf_op jit(solution)/shard_map/reduce_scatter | solution.py:70
  297.4 2.5 multiply_convert_fusion
  299.9 0.2 reduce-scatter.7.cloned.1.call-start
  300.2 81.2 %all-gather.6.cloned.1.call-done = bf16[512,4096]{1,0:T(8,128)(2,1)} async-done(((bf16[512,1024]{1,0:T(8,128)(2,1)}), bf16[512,4096]{1,0:T(8,128)(2,1)}) %all-gather.6.cloned.1.call-update) | async-done | bytes 4194320 | tf_op jit(solution)/shard_map/all_gather | solution.py:74
  381.4 22.3 %fusion = bf16[3584,4096]{0,1:T(8,128)(2,1)} fusion(bf16[512,4096]{1,0:T(8,128)(2,1)} %all-gather.6.cloned.1.call-done, bf16[512,3584]{1,0:T(8,128)(2,1)} %param.9), kind=kOutput, calls=%fused_computation.3 | convolution fusion | flops 15047065600 | bytes 37224448 | tf_op jit(solution)/shard_map/dot_general | solution.py:77
  403.7 37.0 %copy.44 = bf16[3584,4096]{1,0:T(8,128)(2,1)} copy(bf16[3584,4096]{0,1:T(8,128)(2,1)} %fusion) | data formatting | bytes 58720256
  440.7 16.7 %copy.36 = f32[896,4096]{0,1:T(8,128)} copy(f32[896,4096]{1,0:T(8,128)} %param.11) | data formatting | bytes 29360128 | tf_op args[2]
  458.1 18.0 %copy.39 = f32[896,4096]{0,1:T(8,128)} copy(f32[896,4096]{1,0:T(8,128)} %param.12) | data formatting | bytes 29360128 | tf_op args[3]
  476.1 171.1 %reduce-scatter.7.cloned.1.call-done = bf16[896,4096]{1,0:T(8,128)(2,1)} async-done(((bf16[3584,4096]{1,0:T(8,128)(2,1)}), bf16[896,4096]{1,0:T(8,128)(2,1)}) %reduce-scatter.7.cloned.1.call-update) | async-done | bytes 7340048
  647.2 10.8 copy.45
  658.1 11.6 %multiply_reduce_fusion.1 = f32[]{:T(128)} fusion(f32[896,4096]{0,1:T(8,128)} %copy.36, bf16[896,4096]{0,1:T(8,128)(2,1)} %copy.45, f32[]{:T(128)} %bitcast.22), kind=kLoop, calls=%fused_computation.7 | loop fusion | flops 18350080 | bytes 22020104 | tf_op jit(solution)/shard_map/reduce_sum | solution.py:86
  670.4 32.9 %psum.14 = f32[]{:T(128)} all-reduce(f32[]{:T(128)} %multiply_reduce_fusion.1), channel_id=1, replica_groups=mesh['groups'=2,'flat'=4,'dp'=4] {'flat','dp'}, use_global_device_ids=true, to_apply=%region_3.0 | all-reduce | flops 1 | bytes 8 | tf_op jit(solution)/shard_map/psum | solution.py:86
  703.9 13.4 %multiply_reduce_fusion = f32[]{:T(128)} fusion(f32[896,4096]{0,1:T(8,128)} %copy.39, f32[]{:T(128)} %bitcast.25, f32[896,4096]{0,1:T(8,128)} %copy.36, f32[]{:T(128)} %div.28, f32[]{:T(128)} %bitcast.23, bf16[896,4096]{0,1:T(8,128)(2,1)} %copy.45), kind=kLoop, calls=%fused_computation.5 | loop fusion | flops 33030144 | bytes 36700176 | tf_op jit(solution)/shard_map/reduce_sum | solution.py:88
  717.3 16.1 %copy.40 = s32[896,4096]{0,1:T(8,128)} copy(s32[896,4096]{1,0:T(8,128)} %param.13) | data formatting | bytes 29360128 | tf_op args[4]
  733.4 30.3 %psum.15 = f32[]{:T(128)} all-reduce(f32[]{:T(128)} %multiply_reduce_fusion), channel_id=1, replica_groups=mesh['groups'=2,'flat'=4,'dp'=4] {'flat','dp'}, use_global_device_ids=true, to_apply=%region_5.0 | all-reduce | flops 1 | bytes 8 | tf_op jit(solution)/shard_map/psum | solution.py:88
  764.4 28.3 %convert_multiply_fusion = (f32[896,4096]{0,1:T(8,128)}, f32[896,4096]{0,1:T(8,128)}) fusion(s32[896,4096]{0,1:T(8,128)} %copy.40, f32[]{:T(128)} %sqrt.3, f32[896,4096]{0,1:T(8,128)} %copy.39, f32[]{:T(128)} %bitcast.26, f32[896,4096]{0,1:T(8,128)} %copy.36, f32[]{:T(128)} %div.28, f32[]{:T(128)} %bitcast.24, bf16[896,4096]{0,1:T(8,128)(2,1)} %copy.45), kind=kLoop, calls=%fused_computation.4 | loop fusion | flops 44040192 | bytes 80740368 | tf_op jit(solution)/shard_map/mul | solution.py:92
  792.7 16.1 %copy.41 = f32[896,4096]{1,0:T(8,128)} copy(f32[896,4096]{0,1:T(8,128)} %get-tuple-element.20) | data formatting | bytes 29360128 | tf_op jit(solution)/shard_map/mul | solution.py:92
  808.8 15.8 %reshape.33 = f32[28672,128]{1,0:T(8,128)} reshape(f32[896,4096]{1,0:T(8,128)} %copy.41) | data formatting | bytes 29360128 | tf_op jit(solution)/shard_map/reshape | solution.py:94
  824.6 15.6 %convolution_convert_fusion = bf16[28672,128]{1,0:T(8,128)(2,1)} fusion(f32[28672,128]{1,0:T(8,128)} %reshape.33), kind=kOutput, calls=%fused_computation.1 | convolution fusion | flops 5641240576 | bytes 22020096 | tf_op jit(solution)/shard_map/dot_general | solution.py:94
  840.3 11.8 %convert_element_type.47 = bf16[224,16,1024]{2,1,0:T(8,128)(2,1)} reshape(bf16[28672,128]{1,0:T(8,128)(2,1)} %convolution_convert_fusion) | data formatting | bytes 14680064 | tf_op jit(solution)/shard_map/convert_element_type | solution.py:98
  852.0 10.2 copy.42
  862.2 5.0 all-to-all-start
  867.2 16.1 %copy.43 = f32[896,4096]{1,0:T(8,128)} copy(f32[896,4096]{0,1:T(8,128)} %get-tuple-element.21) | data formatting | bytes 29360128
  883.3 116.0 %all-to-all-done = bf16[224,16,1024]{2,0,1:T(8,128)(2,1)} async-done(((bf16[224,16,1024]{2,0,1:T(8,128)(2,1)}), bf16[224,16,1024]{2,0,1:T(8,128)(2,1)}, u32[]{:S(2)}, u32[]{:S(2)}) %all-to-all-start) | async-done | bytes 7340064 | tf_op jit(solution)/shard_map/all_to_all | solution.py:97
  999.3 12.7 %fusion.1 = f32[28,1024,128]{1,2,0:T(8,128)} fusion(bf16[28,128,1024]{2,1,0:T(8,128)(2,1)} %bitcast.6), kind=kOutput, calls=%fused_computation.12 | convolution fusion | flops 5637570560 | bytes 22020096 | tf_op jit(solution)/shard_map/ri,bic->brc/dot_general | solution.py:32
  1012.0 50.1 %gather_fusion = f32[4096]{0:T(1024)S(1)} fusion(f32[3584,1024]{1,0:T(8,128)} %bitcast.27, s32[4096]{0:T(1024)S(1)} %fusion.5), kind=kCustom, calls=%fused_computation | custom fusion | bytes 65536 | tf_op jit(solution)/shard_map/gather | solution.py:42
  1062.1 48.9 %all-gather = f32[65536]{0:T(1024)S(1)} all-gather(f32[4096]{0:T(1024)S(1)} %and_select_fusion), channel_id=2, replica_groups=mesh['groups'=2,'flat'=4,'dp'=4] {'flat','dp'}, dimensions={0}, use_global_device_ids=true | all-gather | bytes 278528 | tf_op jit(solution)/shard_map/all_gather | solution.py:11
  1111.0 0.1 reshape.42
  1111.0 0.6 reduce_sum.29
  (15 shorter events, 0.2 us)
Async XLA Ops:
  7.2 190.3 %all-gather.4.cloned.1.call-start = ((), (), s32[]{:S(2)}) async-start(), calls=%async_computation.3 | async-start | bytes 36700160 | tf_op jit(solution)/shard_map/all_gather | solution.py:67
  16.6 280.8 %copy-start.2 = (f32[512]{0:T(512)S(1)}, f32[512]{0:T(512)}, u32[]{:S(2)}) copy-start(f32[512]{0:T(512)} %param.10) | copy-start | bytes 6148
  16.6 280.8 %reduce-scatter.5.cloned.1.call-start = ((), (), s32[]{:S(2)}) async-start(), calls=%async_computation.4 | async-start | bytes 5242880 | tf_op jit(solution)/shard_map/reduce_scatter | solution.py:70
  220.5 160.9 %all-gather.6.cloned.1.call-start = ((), (), s32[]{:S(2)}) async-start(), calls=%async_computation.5 | async-start | bytes 5242880 | tf_op jit(solution)/shard_map/all_gather | solution.py:74
  299.9 347.3 %reduce-scatter.7.cloned.1.call-start = ((), (), s32[]{:S(2)}) async-start(), calls=%async_computation.6 | async-start | bytes 36700160
  852.0 15.2 %copy-start = (s32[4096]{0:T(1024)S(1)}, s32[4096]{0:T(1024)}, u32[]{:S(2)}) copy-start(s32[4096]{0:T(1024)} %param.17) | copy-start | bytes 49156
  852.0 15.2 %copy-start.1 = (s32[4096]{0:T(1024)S(1)}, s32[4096]{0:T(1024)}, u32[]{:S(2)}) copy-start(s32[4096]{0:T(1024)} %param.16) | copy-start | bytes 49156
  862.2 137.1 %all-to-all-start = ((bf16[224,16,1024]{2,0,1:T(8,128)(2,1)}), bf16[224,16,1024]{2,0,1:T(8,128)(2,1)}, u32[]{:S(2)}, u32[]{:S(2)}) async-start(bf16[224,16,1024]{2,0,1:T(8,128)(2,1)} %copy.42), calls=%async_computation.1 | async-start | bytes 14680064 | tf_op jit(solution)/shard_map/all_to_all | solution.py:97
Sparse Core Ops, SparseCore 0:
  16.7 180.6 all-gather.3
  220.6 76.7 reduce-scatter.4
  300.1 81.2 all-gather.5
  440.8 206.3 reduce-scatter.6
